TPU v7x, 32 devices: a whole 2x2x4 slice. The times are simulated.
32 devices in a mesh: dp: 4 (over z), seq: 8 (over y, x, core).
Axes of the slice: x: 2, y: 2, z: 4, core: 2. Of those that a mesh axis runs over, the one named last changes fastest.
Arguments:
- tokens: bfloat16 [8, 4096, 512], P('dp', 'seq'), may hold values from -6 to 6
- prefix: int32 [8], P('dp'), may hold values from 409 to 2048
- neighbours: int32 [8, 4096, 4], P('dp', 'seq'), may hold values from 0 to 1023
- table: bfloat16 [1024, 512], P('seq'), may hold values from -6 to 6
- attn_gain: bfloat16 [512], P(('dp', 'seq')), may hold values from 0.5 to 1.5
- w_query: bfloat16 [512, 512], P(('dp', 'seq')), may hold values from -0.25 to 0.25
- w_key: bfloat16 [512, 512], P(('dp', 'seq')), may hold values from -0.25 to 0.25
- w_value: bfloat16 [512, 512], P(('dp', 'seq')), may hold values from -0.25 to 0.25
- gate_vector: bfloat16 [512], P(('dp', 'seq')), may hold values from -6 to 6
- w_output: bfloat16 [512, 512], P(('dp', 'seq')), may hold values from -0.5 to 0.5
- ffn_gain: bfloat16 [512], P(('dp', 'seq')), may hold values from 0.5 to 1.5
- w_inner: bfloat16 [512, 2048], P(('dp', 'seq')), may hold values from -0.25 to 0.25
- w_outer: bfloat16 [2048, 512], P(('dp', 'seq')), may hold values from -0.125 to 0.125
- cotangent: bfloat16 [8, 4096, 512], P('dp', 'seq'), may hold values from -6 to 6
Outputs:
- output: bfloat16 [8, 4096, 512], P('dp', 'seq')
- input_grad: float32 [8, 4096, 512], P('dp', 'seq')
- grad_attn_gain: float32 [512], P(('dp', 'seq'))
- grad_w_query: float32 [512, 512], P(('dp', 'seq'))
- grad_w_key: float32 [512, 512], P(('dp', 'seq'))
- grad_w_value: float32 [512, 512], P(('dp', 'seq'))
- grad_gate_vector: float32 [512], P(('dp', 'seq'))
- grad_w_output: float32 [512, 512], P(('dp', 'seq'))
- grad_ffn_gain: float32 [512], P(('dp', 'seq'))
- grad_w_inner: float32 [512, 2048], P(('dp', 'seq'))
- grad_w_outer: float32 [2048, 512], P(('dp', 'seq'))
All inputs are finite; a program needn't handle non-finite values.
Results may differ from a plain program's by a relative error of at most 0.012.
Values may be sent and summed in bfloat16 or wider, within the bound.
A program may use at most 192 MiB of HBM per device.

v0:
```python
import jax
import jax.numpy as jnp
from jax import lax
from jax.sharding import PartitionSpec as P

D = 512
HEADS = 8
HD = 64
KNN = 4
SEG = 512


epsilon = 1e-06
masked_floor = -1000000000.0


def from_behind(value, axis, by):
    count = lax.axis_size(axis)
    pairs = [(i, i + by) for i in range(count) if 0 <= i + by < count]
    return lax.ppermute(value, axis, pairs)


def times_plain(left, right):
    return jnp.dot(left, right, preferred_element_type=jnp.float32)


def times_first_t(left, right):
    return lax.dot_general(
        left, right, (((0,), (0,)), ((), ())), preferred_element_type=jnp.float32
    )


def times_second_t(left, right):
    return lax.dot_general(
        left, right, (((1,), (1,)), ((), ())), preferred_element_type=jnp.float32
    )


def gelu_tanh(values):
    return jax.nn.gelu(values, approximate=True)


def rms_scale(values):
    return lax.rsqrt(jnp.mean(values * values, axis=-1, keepdims=True) + epsilon)


def norm_back(grad_normed, normed, scale):
    return scale * (grad_normed - normed * jnp.mean(grad_normed * normed, axis=-1, keepdims=True))


def split_heads(rows):
    return rows.reshape(rows.shape[0], HEADS, HD).transpose(1, 0, 2)


def merge_heads(stacked):
    return stacked.transpose(1, 0, 2).reshape(stacked.shape[1], D)


def visible_mask(segment, prefix_len):
    query_pos = segment * SEG + lax.iota(jnp.int32, SEG)
    key_pos = (segment - 1) * SEG + lax.iota(jnp.int32, 2 * SEG)
    return (key_pos[None, :] >= 0) & (
        (key_pos[None, :] <= query_pos[:, None])
        | (query_pos[:, None] < prefix_len) & (key_pos[None, :] < prefix_len)
    )


def fetch_attention(attn_gain, w_query, w_key, w_value, gate_vector, w_output):
    return (
        lax.all_gather(attn_gain, ("dp", "seq"), axis=0, tiled=True),
        lax.all_gather(w_query, ("dp", "seq"), axis=0, tiled=True),
        lax.all_gather(w_key, ("dp", "seq"), axis=0, tiled=True),
        lax.all_gather(w_value, ("dp", "seq"), axis=0, tiled=True),
        lax.all_gather(gate_vector, ("dp", "seq"), axis=0, tiled=True),
        lax.all_gather(w_output, ("dp", "seq"), axis=0, tiled=True),
    )


def fetch_feedforward(ffn_gain, w_inner, w_outer):
    return (
        lax.all_gather(ffn_gain, ("dp", "seq"), axis=0, tiled=True),
        lax.all_gather(w_inner, ("dp", "seq"), axis=0, tiled=True),
        lax.all_gather(w_outer, ("dp", "seq"), axis=0, tiled=True),
    )


def forward_pass(tokens_row, visible, near_b, attn_set, ffn_set):
    attn_gain, w_query, w_key, w_value, gate_vector, w_output = attn_set
    ffn_gain, w_inner, w_outer = ffn_set
    rows_count = tokens_row.shape[0]
    inputs_f = tokens_row.astype(jnp.float32)
    scale_one = rms_scale(inputs_f)
    normed_one = inputs_f * scale_one
    normed_in = (normed_one * attn_gain.astype(jnp.float32)).astype(jnp.bfloat16)
    query_b = times_plain(normed_in, w_query).astype(jnp.bfloat16)
    key_b = times_plain(normed_in, w_key).astype(jnp.bfloat16)
    value_b = times_plain(normed_in, w_value).astype(jnp.bfloat16)
    key_prev, value_prev = from_behind((key_b, value_b), "seq", 1)
    key_all = jnp.concatenate([key_prev, key_b], axis=0)
    value_all = jnp.concatenate([value_prev, value_b], axis=0)
    visible_f = visible.astype(jnp.float32)

    def head_forward(operands):
        query_h, key_h, value_h = operands
        scores = jnp.where(visible, times_second_t(query_h, key_h) * 0.125, masked_floor)
        row_max = jnp.max(scores, axis=1, keepdims=True)
        exponent = jnp.exp(scores - row_max) * visible_f
        row_sum = jnp.sum(exponent, axis=1, keepdims=True)
        attn_probs = (exponent / row_sum).astype(jnp.bfloat16)
        return (times_plain(attn_probs, value_h), (row_max + jnp.log(row_sum))[:, 0])

    local_h, log_norm = lax.map(
        head_forward, (split_heads(query_b), split_heads(key_all), split_heads(value_all))
    )
    local_t = local_h.transpose(1, 0, 2)
    query_t = query_b.reshape(rows_count, HEADS, HD)
    near_scores = (
        jnp.einsum("shd,skhd->shk", query_t, near_b, preferred_element_type=jnp.float32) * 0.125
    )
    near_exp = jnp.exp(near_scores - jnp.max(near_scores, axis=-1, keepdims=True))
    near_weights = near_exp / jnp.sum(near_exp, axis=-1, keepdims=True)
    recalled = jnp.einsum("shk,skhd->shd", near_weights, near_b, preferred_element_type=jnp.float32)
    gate_h = gate_vector.astype(jnp.float32).reshape(HEADS, HD)
    gate_open = jax.nn.sigmoid(jnp.sum(local_t * gate_h, axis=-1, keepdims=True))
    blended_b = (
        (gate_open * recalled + (1.0 - gate_open) * local_t)
        .reshape(rows_count, D)
        .astype(jnp.bfloat16)
    )
    middle = inputs_f + times_plain(blended_b, w_output)
    scale_two = rms_scale(middle)
    normed_two = middle * scale_two
    ffn_in = (normed_two * ffn_gain.astype(jnp.float32)).astype(jnp.bfloat16)
    hidden_pre = times_plain(ffn_in, w_inner)
    hidden_b = gelu_tanh(hidden_pre).astype(jnp.bfloat16)
    result = (middle + times_plain(hidden_b, w_outer)).astype(jnp.bfloat16)
    kept = (
        scale_one,
        normed_one,
        normed_in,
        query_b,
        key_all,
        value_all,
        log_norm,
        local_t,
        near_weights,
        recalled,
        gate_open,
        blended_b,
        scale_two,
        normed_two,
        ffn_in,
        hidden_pre,
        hidden_b,
    )
    return (result, kept)


def backward_pass(kept, cot_row, visible, near_b, attn_set, ffn_set):
    (
        scale_one,
        normed_one,
        normed_in,
        query_b,
        key_all,
        value_all,
        log_norm,
        local_t,
        near_weights,
        recalled,
        gate_open,
        blended_b,
        scale_two,
        normed_two,
        ffn_in,
        hidden_pre,
        hidden_b,
    ) = kept
    attn_gain, w_query, w_key, w_value, gate_vector, w_output = attn_set
    ffn_gain, w_inner, w_outer = ffn_set
    rows_count = cot_row.shape[0]
    dout = cot_row.astype(jnp.float32)
    grad_outer = times_first_t(hidden_b, cot_row)
    grad_hidden = times_second_t(cot_row, w_outer)
    unused_value, gelu_pull = jax.vjp(gelu_tanh, hidden_pre)
    grad_pre = gelu_pull(grad_hidden)[0].astype(jnp.bfloat16)
    grad_inner = times_first_t(ffn_in, grad_pre)
    grad_ffn_in = times_second_t(grad_pre, w_inner)
    grad_ffn_gain = jnp.sum(grad_ffn_in * normed_two, axis=0)
    grad_middle = dout + norm_back(
        grad_ffn_in * ffn_gain.astype(jnp.float32), normed_two, scale_two
    )
    grad_branch_b = grad_middle.astype(jnp.bfloat16)
    grad_output = times_first_t(blended_b, grad_branch_b)
    grad_blended = times_second_t(grad_branch_b, w_output).reshape(rows_count, HEADS, HD)
    gate_h = gate_vector.astype(jnp.float32).reshape(HEADS, HD)
    grad_recalled = gate_open * grad_blended
    grad_gate = (
        jnp.sum(grad_blended * (recalled - local_t), axis=-1, keepdims=True)
        * gate_open
        * (1.0 - gate_open)
    )
    grad_gate_vector = jnp.sum(grad_gate * local_t, axis=0).reshape(D)
    grad_local_b = (
        ((1.0 - gate_open) * grad_blended + grad_gate * gate_h)
        .astype(jnp.bfloat16)
        .transpose(1, 0, 2)
    )
    grad_near_w = jnp.einsum(
        "shd,skhd->shk", grad_recalled, near_b, preferred_element_type=jnp.float32
    )
    grad_near = near_weights * (
        grad_near_w - jnp.sum(near_weights * grad_near_w, axis=-1, keepdims=True)
    )
    grad_query_near = (
        jnp.einsum("shk,skhd->shd", grad_near, near_b, preferred_element_type=jnp.float32) * 0.125
    )
    visible_f = visible.astype(jnp.float32)

    def head_backward(operands):
        query_h, key_h, value_h, grad_h, norm_h = operands
        scores = jnp.where(visible, times_second_t(query_h, key_h) * 0.125, masked_floor)
        attn_probs = jnp.exp(scores - norm_h[:, None]) * visible_f
        grad_probs = times_second_t(grad_h, value_h)
        grad_scores = (
            attn_probs * (grad_probs - jnp.sum(attn_probs * grad_probs, axis=1, keepdims=True))
        ).astype(jnp.bfloat16)
        return (
            times_plain(grad_scores, key_h) * 0.125,
            times_first_t(grad_scores, query_h) * 0.125,
            times_first_t(attn_probs.astype(jnp.bfloat16), grad_h),
        )

    grad_query_h, grad_key_h, grad_value_h = lax.map(
        head_backward,
        (
            split_heads(query_b),
            split_heads(key_all),
            split_heads(value_all),
            grad_local_b,
            log_norm,
        ),
    )
    grad_key_all = merge_heads(grad_key_h)
    grad_value_all = merge_heads(grad_value_h)
    later_key, later_value = (
        from_behind(grad_key_all[:rows_count].astype(jnp.bfloat16), "seq", -1).astype(jnp.float32),
        from_behind(grad_value_all[:rows_count].astype(jnp.bfloat16), "seq", -1).astype(
            jnp.float32
        ),
    )
    grad_query_b = (merge_heads(grad_query_h) + grad_query_near.reshape(rows_count, D)).astype(
        jnp.bfloat16
    )
    grad_key_b = (grad_key_all[rows_count:] + later_key).astype(jnp.bfloat16)
    grad_value_b = (grad_value_all[rows_count:] + later_value).astype(jnp.bfloat16)
    grad_query = times_first_t(normed_in, grad_query_b)
    grad_key = times_first_t(normed_in, grad_key_b)
    grad_value = times_first_t(normed_in, grad_value_b)
    grad_normed_in = (
        times_second_t(grad_query_b, w_query)
        + times_second_t(grad_key_b, w_key)
        + times_second_t(grad_value_b, w_value)
    )
    grad_attn_gain = jnp.sum(grad_normed_in * normed_one, axis=0)
    input_grad = grad_middle + norm_back(
        grad_normed_in * attn_gain.astype(jnp.float32), normed_one, scale_one
    )
    grads = (
        grad_attn_gain,
        grad_query,
        grad_key,
        grad_value,
        grad_gate_vector,
        grad_output,
        grad_ffn_gain,
        grad_inner,
        grad_outer,
    )
    return (grads, input_grad)


def local(
    tokens,
    prefix,
    neighbours,
    table,
    attn_gain,
    w_query,
    w_key,
    w_value,
    gate_vector,
    w_output,
    ffn_gain,
    w_inner,
    w_outer,
    cotangent,
):
    full_table = lax.all_gather(table, "seq", axis=0, tiled=True)
    segment = lax.axis_index("seq")
    rows_count = tokens.shape[1]
    outputs = []
    input_grads = []
    running = ()
    for micro_batch in range(tokens.shape[0]):
        visible = visible_mask(segment, prefix[micro_batch])
        near_b = jnp.take(full_table, neighbours[micro_batch].reshape(-1), axis=0).reshape(
            rows_count, KNN, HEADS, HD
        )
        attn_fwd = fetch_attention(attn_gain, w_query, w_key, w_value, gate_vector, w_output)
        ffn_fwd = fetch_feedforward(ffn_gain, w_inner, w_outer)
        result, kept = forward_pass(tokens[micro_batch], visible, near_b, attn_fwd, ffn_fwd)
        attn_back = fetch_attention(attn_gain, w_query, w_key, w_value, gate_vector, w_output)
        ffn_back = fetch_feedforward(ffn_gain, w_inner, w_outer)
        grads, input_grad = backward_pass(
            kept, cotangent[micro_batch], visible, near_b, attn_back, ffn_back
        )
        if micro_batch == 0:
            running = grads
        else:
            running = tuple((earlier + increment for earlier, increment in zip(running, grads)))
        outputs.append(result)
        input_grads.append(input_grad)
    shares = lax.psum_scatter(running, ("dp", "seq"), scatter_dimension=0, tiled=True)
    return (
        jnp.stack(outputs),
        jnp.stack(input_grads),
        shares[0],
        shares[1],
        shares[2],
        shares[3],
        shares[4],
        shares[5],
        shares[6],
        shares[7],
        shares[8],
    )


def solution(mesh):
    return jax.shard_map(
        local,
        mesh=mesh,
        in_specs=(
            P("dp", "seq", None),
            P("dp"),
            P("dp", "seq", None),
            P("seq", None),
            P(("dp", "seq")),
            P(("dp", "seq"), None),
            P(("dp", "seq"), None),
            P(("dp", "seq"), None),
            P(("dp", "seq")),
            P(("dp", "seq"), None),
            P(("dp", "seq")),
            P(("dp", "seq"), None),
            P(("dp", "seq"), None),
            P("dp", "seq", None),
        ),
        out_specs=(
            P("dp", "seq", None),
            P("dp", "seq", None),
            P(("dp", "seq")),
            P(("dp", "seq"), None),
            P(("dp", "seq"), None),
            P(("dp", "seq"), None),
            P(("dp", "seq")),
            P(("dp", "seq"), None),
            P(("dp", "seq")),
            P(("dp", "seq"), None),
            P(("dp", "seq"), None),
        ),
        check_vma=False,
    )
```

profile of v0, /device:TPU:0, one launch (start us, length us, event | category | flops | bytes accessed | tf_op | source)
XLA Modules:
  0.0 1372.2 jit_solution(6506342017849975278)
XLA Ops:
  11.3 42.0 %all-reduce.7 = (bf16[512]{0:T(512)(128)(2,1)S(1)}, bf16[512]{0:T(512)(128)(2,1)S(1)}, bf16[512]{0:T(512)(128)(2,1)S(1)}) all-reduce(bf16[512]{0:T(512)(128)(2,1)S(1)} %dynamic-update-slice.1, bf16[512]{0:T(512)(128)(2,1)S(1)} %dynamic-update-slice, bf16[512]{0:T(512)(128)(2,1)S(1)} %dynamic-update-slice.2), channel_id=1, replica_groups=mesh['dp'=4,'seq'=8] {'dp','seq'}, use_global_device_ids=true, to_apply=%add.1 | all-reduce | flops 1536 | bytes 6144
  53.7 42.1 %all_gather.22 = bf16[512,512]{1,0:T(8,128)(2,1)S(1)} all-gather(bf16[16,512]{1,0:T(8,128)(2,1)S(1)} %copy-done.72), channel_id=1, replica_groups=mesh['dp'=4,'seq'=8] {'dp','seq'}, dimensions={0}, use_global_device_ids=true | all-gather | bytes 540672 | tf_op jit(solution)/shard_map/all_gather | solution.py:72
  100.1 37.7 %all_gather.23 = bf16[512,512]{1,0:T(8,128)(2,1)S(1)} all-gather(bf16[16,512]{1,0:T(8,128)(2,1)S(1)} %copy-done.73), channel_id=1, replica_groups=mesh['dp'=4,'seq'=8] {'dp','seq'}, dimensions={0}, use_global_device_ids=true | all-gather | bytes 540672 | tf_op jit(solution)/shard_map/all_gather | solution.py:73
  151.1 40.8 %all_gather.21 = bf16[512,512]{1,0:T(8,128)(2,1)S(1)} all-gather(bf16[16,512]{1,0:T(8,128)(2,1)S(1)} %copy-done.74), channel_id=1, replica_groups=mesh['dp'=4,'seq'=8] {'dp','seq'}, dimensions={0}, use_global_device_ids=true | all-gather | bytes 540672 | tf_op jit(solution)/shard_map/all_gather | solution.py:71
  207.1 41.2 %all_gather.26 = bf16[512,512]{1,0:T(8,128)(2,1)} all-gather(bf16[16,512]{1,0:T(8,128)(2,1)S(1)} %copy-done.75), channel_id=1, replica_groups=mesh['dp'=4,'seq'=8] {'dp','seq'}, dimensions={0}, use_global_device_ids=true | all-gather | bytes 540672 | tf_op jit(solution)/shard_map/all_gather | solution.py:75
  256.6 46.4 %while.60 = (s32[]{:T(128)}, f32[8,512,64]{1,2,0:T(8,128)}, f32[8,512]{1,0:T(8,128)S(1)}, bf16[8,512,64]{2,1,0:T(8,128)(2,1)}, bf16[8,1024,64]{2,1,0:T(8,128)(2,...) while((s32[]{:T(128)}, f32[8,512,64]{1,2,0:T(8,128)}, ...), condition=%wide.region_4.5_spmd.clone.clone, body=%wide.region_1.0_spmd.clone.clone.sunk | while | flops 147848704 | bytes 7126657 | solution.py:112
  311.3 46.4 %while.61 = (s32[]{:T(128)}, f32[8,512,64]{1,2,0:T(8,128)}, f32[8,512]{1,0:T(8,128)S(1)}, bf16[8,512,64]{2,1,0:T(8,128)(2,1)}, bf16[8,1024,64]{2,1,0:T(8,128)(2,...) while((s32[]{:T(128)}, f32[8,512,64]{1,2,0:T(8,128)}, ...), condition=%wide.region_13.15_spmd.clone.clone, body=%wide.region_10.14_spmd.clone.clone.sunk | while | flops 147848704 | bytes 7126657 | solution.py:112
  360.3 9.0 gather_fusion
  370.8 6.5 reshape.316
  377.3 5.7 fusion.98
  385.0 6.8 fusion.100
  391.8 9.2 gather_fusion.1
  405.9 6.5 reshape.320
  412.4 5.4 fusion.102
  418.6 6.9 fusion.104
  432.5 5.3 fusion.215
  437.7 6.4 fusion.112
  470.1 78.9 %while.62 = (s32[]{:T(128)}, f32[8,512,64]{1,2,0:T(8,128)}, f32[8,1024,64]{1,2,0:T(8,128)}, f32[8,1024,64]{1,2,0:T(8,128)}, bf16[8,512,64]{2,1,0:T(8,128)(2,1)},...) while((s32[]{:T(128)}, f32[8,512,64]{1,2,0:T(8,128)}, ...), condition=%wide.region_22.24_spmd.clone.clone, body=%wide.region_20.23_spmd.clone.clone.sunk | while | flops 342982144 | bytes 17587856 | solution.py:234
  555.6 84.5 %while.63 = (s32[]{:T(128)}, f32[8,512,64]{1,2,0:T(8,128)}, f32[8,1024,64]{1,2,0:T(8,128)}, f32[8,1024,64]{1,2,0:T(8,128)}, bf16[8,512,64]{2,1,0:T(8,128)(2,1)},...) while((s32[]{:T(128)}, f32[8,512,64]{1,2,0:T(8,128)}, ...), condition=%wide.region_29.31_spmd.clone.clone, body=%wide.region_27.30_spmd.clone.clone.sunk | while | flops 342982144 | bytes 17587856 | solution.py:234
  642.1 5.4 fusion.99
  648.3 6.9 fusion.101
  660.5 6.4 fusion.103
  669.8 7.0 fusion.105
  703.3 10.5 collective-permute-done.4
  726.8 4.3 fusion.186
  735.9 4.9 fusion.135
  752.5 48.8 %all-reduce.6 = (f32[512]{0:T(512)S(1)}, f32[512]{0:T(512)S(1)}, f32[512]{0:T(512)S(1)}) all-reduce(f32[512]{0:T(512)S(1)} %add.320, f32[512]{0:T(512)S(1)} %add.325, f32[512]{0:T(512)S(1)} %add.327), channel_id=2, replica_groups=mesh['dp'=4,'seq'=8] {'dp','seq'}, use_global_device_ids=true, to_apply=%region_34.36.clone | all-reduce | flops 1536 | bytes 12288
  805.4 13.3 reduce-scatter.7.cloned.1.call-done
  818.7 134.0 %reduce-scatter.11.cloned.1.call-done = f32[16,512]{1,0:T(8,128)} async-done(((f32[512,512]{1,0:T(8,128)}), f32[16,512]{1,0:T(8,128)}) %reduce-scatter.11.cloned.1.call-update) | async-done | bytes 32784 | tf_op jit(solution)/shard_map/reduce_scatter | solution.py:324
  952.6 133.6 %reduce-scatter.9.cloned.1.call-done = f32[16,512]{1,0:T(8,128)} async-done(((f32[512,512]{1,0:T(8,128)}), f32[16,512]{1,0:T(8,128)}) %reduce-scatter.9.cloned.1.call-update) | async-done | bytes 32784 | tf_op jit(solution)/shard_map/reduce_scatter | solution.py:324
  1086.2 139.6 %reduce-scatter.15.cloned.1.call-done = f32[16,2048]{1,0:T(8,128)} async-done(((f32[512,2048]{1,0:T(8,128)}), f32[16,2048]{1,0:T(8,128)}) %reduce-scatter.15.cloned.1.call-update) | async-done | bytes 131088 | tf_op jit(solution)/shard_map/reduce_scatter | solution.py:324
  1225.9 139.6 %reduce-scatter.17.cloned.1.call-done = f32[64,512]{1,0:T(8,128)} async-done(((f32[2048,512]{1,0:T(8,128)}), f32[64,512]{1,0:T(8,128)}) %reduce-scatter.17.cloned.1.call-update) | async-done | bytes 131088 | tf_op jit(solution)/shard_map/reduce_scatter | solution.py:324
  (559 shorter events, 430.8 us)
Async XLA Ops:
  7.2 353.1 %all-gather.4.cloned.1.call-start = ((), (), s32[]{:S(2)}) async-start(), calls=%async_computation.6 | async-start | bytes 1179648 | tf_op jit(solution)/shard_map/all_gather | solution.py:299
  7.9 424.5 %all-gather.6.cloned.1.call-start = ((), (), s32[]{:S(2)}) async-start(), calls=%async_computation.7 | async-start | bytes 2162688 | tf_op jit(solution)/shard_map/all_gather | solution.py:82
  8.7 429.1 %all-gather.8.cloned.1.call-start = ((), (), s32[]{:S(2)}) async-start(), calls=%async_computation.8 | async-start | bytes 2162688 | tf_op jit(solution)/shard_map/all_gather | solution.py:83
  10.0 43.6 %copy-start.72 = (bf16[16,512]{1,0:T(8,128)(2,1)S(1)}, bf16[16,512]{1,0:T(8,128)(2,1)}, u32[]{:S(2)}) copy-start(bf16[16,512]{1,0:T(8,128)(2,1)} %param.30) | copy-start | bytes 49156
  10.5 89.7 %copy-start.73 = (bf16[16,512]{1,0:T(8,128)(2,1)S(1)}, bf16[16,512]{1,0:T(8,128)(2,1)}, u32[]{:S(2)}) copy-start(bf16[16,512]{1,0:T(8,128)(2,1)} %param.31) | copy-start | bytes 49156
  53.3 139.1 %copy-start.58 = (f32[512]{0:T(512)}, f32[512]{0:T(512)S(1)}, u32[]{:S(2)}) copy-start(f32[512]{0:T(512)S(1)} %convert_element_type.204) | copy-start | bytes 6148
  53.6 138.2 %copy-start.60 = (f32[512]{0:T(512)}, f32[512]{0:T(512)S(1)}, u32[]{:S(2)}) copy-start(f32[512]{0:T(512)S(1)} %get-tuple-element.924) | copy-start | bytes 6148
  53.6 138.8 %copy-start.62 = (f32[512]{0:T(512)}, f32[512]{0:T(512)S(1)}, u32[]{:S(2)}) copy-start(f32[512]{0:T(512)S(1)} %get-tuple-element.923) | copy-start | bytes 6148
  95.8 51.6 %copy-start.37 = (bf16[512,512]{1,0:T(8,128)(2,1)}, bf16[512,512]{1,0:T(8,128)(2,1)S(1)}, u32[]{:S(2)}) copy-start(bf16[512,512]{1,0:T(8,128)(2,1)S(1)} %all_gather.22) | copy-start | bytes 1572868
  97.1 151.1 %collective-permute-start = (bf16[512,512]{1,0:T(8,128)(2,1)}, bf16[512,512]{1,0:T(8,128)(2,1)}, u32[]{:S(2)}, u32[]{:S(2)}) collective-permute-start(bf16[512,512]{1,0:T(8,128)(2,1)} %convolution_convert_fusion.4), channel_id=1, source_target_pairs={{0,1},{1,2},{2,3},{3,4},{4,5},{5,6},{6,7},{8,9},{9,10},{10,11},{11... | collective-permute-start | bytes 1572872 | tf_op jit(solution)/shard_map/ppermute | solution.py:20
  139.3 112.6 %collective-permute-start.1 = (bf16[512,512]{1,0:T(8,128)(2,1)}, bf16[512,512]{1,0:T(8,128)(2,1)}, u32[]{:S(2)}, u32[]{:S(2)}) collective-permute-start(bf16[512,512]{1,0:T(8,128)(2,1)} %convolution_convert_fusion.3), channel_id=1, source_target_pairs={{0,1},{1,2},{2,3},{3,4},{4,5},{5,6},{6,7},{8,9},{9,10},{10,11},{11... | collective-permute-start | bytes 1572872 | tf_op jit(solution)/shard_map/ppermute | solution.py:20
  142.4 8.7 copy-start.74
  143.7 159.3 %collective-permute-start.3 = (bf16[512,512]{1,0:T(8,128)(2,1)}, bf16[512,512]{1,0:T(8,128)(2,1)}, u32[]{:S(2)}, u32[]{:S(2)}) collective-permute-start(bf16[512,512]{1,0:T(8,128)(2,1)} %convolution_convert_fusion), channel_id=1, source_target_pairs={{0,1},{1,2},{2,3},{3,4},{4,5},{5,6},{6,7},{8,9},{9,10},{10,11},{11... | collective-permute-start | bytes 1572872 | tf_op jit(solution)/shard_map/ppermute | solution.py:20
  148.7 157.9 %collective-permute-start.2 = (bf16[512,512]{1,0:T(8,128)(2,1)}, bf16[512,512]{1,0:T(8,128)(2,1)}, u32[]{:S(2)}, u32[]{:S(2)}) collective-permute-start(bf16[512,512]{1,0:T(8,128)(2,1)} %convolution_convert_fusion.1), channel_id=1, source_target_pairs={{0,1},{1,2},{2,3},{3,4},{4,5},{5,6},{6,7},{8,9},{9,10},{10,11},{11... | collective-permute-start | bytes 1572872 | tf_op jit(solution)/shard_map/ppermute | solution.py:20
  151.0 654.3 %reduce-scatter.13.cloned.1.call-start = ((), (), s32[]{:S(2)}) async-start(), calls=%async_computation.12 | async-start | bytes 1081344 | tf_op jit(solution)/shard_map/reduce_scatter | solution.py:324
  357.7 11.5 copy-start.67
  370.8 6.5 copy-start.18
  385.0 6.8 copy-start
  405.9 22.9 %copy-start.14 = (f32[512,8,64]{0,2,1:T(8,128)}, f32[512,8,64]{0,2,1:T(8,128)S(1)}, u32[]{:S(2)}) copy-start(f32[512,8,64]{0,2,1:T(8,128)S(1)} %copy.177) | copy-start | bytes 3145732
  437.7 6.4 copy-start.8
  462.9 355.8 %reduce-scatter.7.cloned.1.call-start = ((), (), s32[]{:S(2)}) async-start(), calls=%async_computation.9 | async-start | bytes 1081344 | tf_op jit(solution)/shard_map/reduce_scatter | solution.py:324
  470.1 78.9 %copy-start.4 = (f32[8,512,64]{1,2,0:T(8,128)S(1)}, f32[8,512,64]{1,2,0:T(8,128)}, u32[]{:S(2)}) copy-start(f32[8,512,64]{1,2,0:T(8,128)} %get-tuple-element.217) | copy-start | bytes 3145732
  555.6 84.6 %copy-start.51 = (f32[512,8,64]{0,2,1:T(8,128)S(1)}, f32[512,8,64]{0,2,1:T(8,128)}, u32[]{:S(2)}) copy-start(f32[512,8,64]{0,2,1:T(8,128)} %get-tuple-element.888) | copy-start | bytes 3145732
  685.9 266.7 %reduce-scatter.11.cloned.1.call-start = ((), (), s32[]{:S(2)}) async-start(), calls=%async_computation.11 | async-start | bytes 1081344 | tf_op jit(solution)/shard_map/reduce_scatter | solution.py:324
  687.4 4.3 collective-permute-start.5
  690.1 4.4 collective-permute-start.7
  697.6 388.7 %reduce-scatter.9.cloned.1.call-start = ((), (), s32[]{:S(2)}) async-start(), calls=%async_computation.10 | async-start | bytes 1081344 | tf_op jit(solution)/shard_map/reduce_scatter | solution.py:324
  699.1 14.7 %collective-permute-start.4 = (bf16[512,512]{0,1:T(8,128)(2,1)S(1)}, bf16[512,512]{0,1:T(8,128)(2,1)S(1)}, u32[]{:S(2)}, u32[]{:S(2)}) collective-permute-start(bf16[512,512]{0,1:T(8,128)(2,1)S(1)} %bitcast.482), channel_id=1, source_target_pairs={{1,0},{2,1},{3,2},{4,3},{5,4},{6,5},{7,6},{9,8},{10,9},{11,10},{12... | collective-permute-start | bytes 1572872 | tf_op jit(solution)/shard_map/ppermute | solution.py:20
  701.8 15.2 %collective-permute-start.6 = (bf16[512,512]{0,1:T(8,128)(2,1)S(1)}, bf16[512,512]{0,1:T(8,128)(2,1)S(1)}, u32[]{:S(2)}, u32[]{:S(2)}) collective-permute-start(bf16[512,512]{0,1:T(8,128)(2,1)S(1)} %bitcast.481), channel_id=1, source_target_pairs={{1,0},{2,1},{3,2},{4,3},{5,4},{6,5},{7,6},{9,8},{10,9},{11,10},{12... | collective-permute-start | bytes 1572872 | tf_op jit(solution)/shard_map/ppermute | solution.py:20
  720.0 505.8 %reduce-scatter.15.cloned.1.call-start = ((), (), s32[]{:S(2)}) async-start(), calls=%async_computation.13 | async-start | bytes 4325376 | tf_op jit(solution)/shard_map/reduce_scatter | solution.py:324
  726.5 638.9 %reduce-scatter.17.cloned.1.call-start = ((), (), s32[]{:S(2)}) async-start(), calls=%async_computation.14 | async-start | bytes 4325376 | tf_op jit(solution)/shard_map/reduce_scatter | solution.py:324
  751.0 52.1 %copy-start.11 = (f32[512,512]{0,1:T(8,128)S(1)}, f32[512,512]{0,1:T(8,128)}, u32[]{:S(2)}) copy-start(f32[512,512]{0,1:T(8,128)} %copy-done.10) | copy-start | bytes 3145732
  (70 other events, 177.9 us)
Sparse Core Ops, SparseCore 0:
  9.9 26.2 all-gather.3
  39.1 57.1 all-gather.5
  151.1 52.8 all-gather.7
  463.0 132.4 reduce-scatter.12
  686.0 132.5 reduce-scatter.6
  821.3 131.2 reduce-scatter.10
  955.5 130.6 reduce-scatter.8
  1089.1 136.7 reduce-scatter.14
  1228.7 136.6 reduce-scatter.16
where the time goes:
time: 1380 us; the launch traced here: 1370 us
  waiting for transfers between devices  578 us (42%)
  matrix products  293 us (21%)
  blocking collectives  253 us (18%)
  local copies, waits for them, and re-layouts  116 us (8%)
  other arithmetic  99 us (7%)
  starting transfers between devices  18 us (1%)
  between operations  15.4 us (1%)
    reduce_scatter x6, waiting for transfers between devices, local(): lax.psum_scatter(running, ('dp', 'seq'), scatter_dimension=0, tiled=True)  560 us
    dot_general x60, matrix products, times_second_t(): lax.dot_general(left, right, (((1,), (1,)), ((), ())), preferred_element_...  110 us
    dot_general x44, matrix products, times_plain(): return jnp.dot(left, right, preferred_element_type=jnp.float32)  99.7 us
    unnamed x2, blocking collectives  90.8 us
    dot_general x44, matrix products, times_first_t(): lax.dot_general(left, right, (((0,), (0,)), ((), ())), preferred_element_...  83.7 us
    unnamed x8, other arithmetic  50.3 us
    all_gather x1, blocking collectives, fetch_attention(): lax.all_gather(w_key, ('dp', 'seq'), axis=0, tiled=True)  42.1 us
    all_gather x1, blocking collectives, fetch_attention(): lax.all_gather(w_output, ('dp', 'seq'), axis=0, tiled=True)  41.2 us
  transfers between devices with their start and end apart: 17, of which 8 were waited for; matrix products, arithmetic and copies ran while one was open for 35% of the time, Pallas kernels for 0%

commit v1 on v0

--- a/solution.py
+++ b/solution.py
@@ -1,6 +1,8 @@
 import jax
 import jax.numpy as jnp
 from jax import lax
+from jax.experimental import pallas as pl
+from jax.experimental.pallas import tpu as pltpu
 from jax.sharding import PartitionSpec as P
 
 D = 512
@@ -8,9 +10,693 @@
 HD = 64
 KNN = 4
 SEG = 512
-
+FF = 2048
+PAIRS = 4
+NB = 2
+MESH = pl.DeviceIdType.MESH
 
 epsilon = 1e-06
+far = 1e30
+f32 = jnp.float32
+bf16 = jnp.bfloat16
+
+
+def mm(left, right, over_left, over_right):
+    return lax.dot_general(
+        left, right, (((over_left,), (over_right,)), ((), ())), preferred_element_type=f32
+    )
+
+
+class Place:
+    def __init__(self, dpn):
+        self.dpn = dpn
+        self.dp = lax.axis_index("dp")
+        self.s = lax.axis_index("seq")
+        self.c = self.s % 2
+        self.x = (self.s // 2) % 2
+        self.y = self.s // 4
+
+    def across(self, axis):
+        if axis == "c":
+            return (self.dp, self.s + 1 - 2 * self.c)
+        if axis == "x":
+            return (self.dp, self.s + 2 * (1 - 2 * self.x))
+        return (self.dp, self.s + 4 * (1 - 2 * self.y))
+
+    def along(self, step):
+        return ((self.dp + step) % self.dpn, self.s)
+
+
+def remote(src, dst, send, recv, device):
+    return pltpu.make_async_remote_copy(
+        src_ref=src, dst_ref=dst, send_sem=send, recv_sem=recv, device_id=device, device_id_type=MESH
+    )
+
+
+class Gather:
+    def __init__(self, place, buf, send, recv, order, flat=False):
+        self.place, self.buf, self.send, self.recv = place, buf, send, recv
+        self.order = order if flat else ("z",) + order
+        self.flat = flat
+        self.live = []
+
+    def copies(self, stage):
+        p = self.place
+        axis = self.order[stage]
+        if axis == "z":
+            own = self.buf.at[p.dp, p.y, p.x, p.c]
+            return [
+                remote(own, own, self.send.at[k], self.recv.at[k], p.along(k + 1))
+                for k in range(p.dpn - 1)
+            ]
+        done = self.order[:stage]
+        part = tuple(slice(None) if n in done else v for n, v in (("y", p.y), ("x", p.x), ("c", p.c)))
+        view = self.buf.at[part] if self.flat else self.buf.at[(slice(None),) + part]
+        slot = (0 if self.flat else p.dpn - 2) + stage
+        return [remote(view, view, self.send.at[slot], self.recv.at[slot], p.across(axis))]
+
+    def start(self, stage):
+        for copy in self.copies(stage):
+            copy.start()
+
+    def step(self, stage):
+        for copy in self.copies(stage):
+            copy.wait_recv()
+        if stage + 1 < len(self.order):
+            self.start(stage + 1)
+
+    def drain(self):
+        for stage in range(len(self.order)):
+            for copy in self.copies(stage):
+                copy.wait_send()
+
+
+class Scatter:
+    def __init__(self, place, acc, recvs, send, recv, order):
+        self.place, self.acc, self.recvs, self.send, self.recv = place, acc, recvs, send, recv
+        self.order = order + ("z",)
+
+    def view(self, stage, other):
+        p = self.place
+        done = self.order[:stage]
+        here = {"y": p.y, "x": p.x, "c": p.c}
+        part = []
+        for name in ("y", "x", "c"):
+            if name == self.order[stage]:
+                part.append(1 - here[name] if other else here[name])
+            elif name in done:
+                part.append(here[name])
+            else:
+                part.append(slice(None))
+        return (slice(None),) + tuple(part)
+
+    def copies(self, stage):
+        p = self.place
+        if stage == 3:
+            rest = (p.y, p.x, p.c)
+            return [
+                remote(
+                    self.acc.at[((p.dp + k + 1) % p.dpn,) + rest],
+                    self.recvs[3].at[k],
+                    self.send.at[3 + k],
+                    self.recv.at[3 + k],
+                    p.along(k + 1),
+                )
+                for k in range(p.dpn - 1)
+            ]
+        return [
+            remote(
+                self.acc.at[self.view(stage, True)],
+                self.recvs[stage],
+                self.send.at[stage],
+                self.recv.at[stage],
+                p.across(self.order[stage]),
+            )
+        ]
+
+    def start(self, stage):
+        for copy in self.copies(stage):
+            copy.start()
+
+    def step(self, stage):
+        for copy in self.copies(stage):
+            copy.wait_recv()
+        where = self.view(stage, False)
+        self.acc[where] = self.acc[where] + self.recvs[stage][...]
+        self.start(stage + 1)
+
+    def total(self):
+        p = self.place
+        for copy in self.copies(3):
+            copy.wait_recv()
+        result = self.acc[p.dp, p.y, p.x, p.c].astype(f32)
+        for k in range(p.dpn - 1):
+            result = result + self.recvs[3][k].astype(f32)
+        return result
+
+    def drain(self):
+        for stage in range(4):
+            for copy in self.copies(stage):
+                copy.wait_send()
+
+
+def heads_of(value):
+    return value.reshape(HEADS, HD, value.shape[-1])
+
+
+def per_head(value):
+    return jnp.sum(heads_of(value), axis=1)
+
+
+def spread(rows):
+    return jnp.broadcast_to(rows[:, None, :], (HEADS, HD, rows.shape[-1])).reshape(D, rows.shape[-1])
+
+
+def norm_scale(value):
+    return lax.rsqrt(jnp.mean(value * value, axis=0, keepdims=True) + epsilon)
+
+
+def norm_back(grad, normed, scale):
+    return scale * (grad - normed * jnp.mean(grad * normed, axis=0, keepdims=True))
+
+
+def one_head(pair, e):
+    row = lax.broadcasted_iota(jnp.int32, pair.shape, 0)
+    return jnp.where((row >= HD) == (e == 1), pair, jnp.zeros_like(pair))
+
+
+def layer(dpn, *refs):
+    (tok, pre, nbr, tab, gains, wq, wk, wv, wo, wi, wu, cot) = refs[:12]
+    (out, ig, gq, gk, gv, go_, gi, gu, gg) = refs[12:21]
+    (
+        bufA, bufB, bufO, bufI, bufU, bufT, tokP, stage, xT, coT, niO, niP, qs, kvO, kvP, loc, near,
+        nw, gate, lse, dlt, mid, bld, fi, y, gm, bias, G3, Gp, accQ, hgR,
+        rI0, rI1, rI2, rI3, rU0, rU1, rU2, rU3, rO0, rO1, rO2, rO3, rQ0, rQ1, rQ2, rQ3,
+        ags, agr, rss, rsr, hs, hr, dms,
+    ) = refs[21:]
+    place = Place(dpn)
+    dp, s = place.dp, place.s
+    cy, cx, cc = place.y, place.x, place.c
+    nseq = 8
+    nxt = (dp, (s + 1) % nseq)
+    prv = (dp, (s + nseq - 1) % nseq)
+
+    tok_in = [pltpu.make_async_copy(tok.at[b], stage.at[b], dms.at[b]) for b in range(NB)]
+    for copy in tok_in:
+        copy.start()
+    for p in range(PAIRS):
+        to = bufA if p < 2 else bufB
+        for i, w in enumerate((wq, wk, wv)):
+            at = (p % 2) * 384 + i * 128
+            to[dp, cy, cx, cc, :, at : at + 128] = w[:, p * 128 : (p + 1) * 128]
+    bufA[dp, cy, cx, cc, :, 768:896] = gains[...]
+    bufO[dp, cy, cx, cc, :, 0:512] = wo[...]
+    bufO[dp, cy, cx, cc, :, 512:640] = gains[...]
+    bufI[dp, cy, cx, cc] = wi[...]
+    bufU[dp, cy, cx, cc] = wu[...]
+    bufT[cy, cx, cc] = tab[...]
+
+    barrier = pltpu.get_barrier_semaphore()
+    greet = [place.along(k + 1) for k in range(dpn - 1)]
+    greet += [place.across("y"), place.across("x"), place.across("c"), nxt, prv]
+    for device in greet:
+        pl.semaphore_signal(barrier, inc=1, device_id=device, device_id_type=MESH)
+    pl.semaphore_wait(barrier, len(greet))
+
+    ag = [
+        Gather(place, bufA, ags.at[0], agr.at[0], ("y", "x", "c")),
+        Gather(place, bufB, ags.at[1], agr.at[1], ("x", "y", "c")),
+        Gather(place, bufT, ags.at[2], agr.at[2], ("y", "x", "c"), flat=True),
+        Gather(place, bufO, ags.at[3], agr.at[3], ("x", "y", "c")),
+        Gather(place, bufI, ags.at[4], agr.at[4], ("y", "x", "c")),
+        Gather(place, bufU, ags.at[5], agr.at[5], ("x", "y", "c")),
+    ]
+    A, B, T, O, I, U = ag
+    halo = [remote(tok.at[b], tokP.at[b], hs.at[b], hr.at[b], nxt) for b in range(NB)]
+    back = [remote(tokP.at[b], hgR.at[b], hs.at[2 + b], hr.at[2 + b], prv) for b in range(NB)]
+
+    A.start(0)
+    B.start(0)
+    halo[0].start()
+
+    seg = s
+    base = seg * SEG
+    away = (seg == 0).astype(f32) * far
+
+    def set_bias(b):
+        q = lax.broadcasted_iota(jnp.int32, (1, SEG), 1)
+        k = lax.broadcasted_iota(jnp.int32, (SEG, SEG), 0)
+        limit = jnp.where(base + q < pre[b], jnp.maximum(q, pre[b] - 1 - base), q)
+        bias[b] = jnp.where(k <= limit, 0.0, -far).astype(f32)
+
+    for copy in tok_in:
+        copy.wait()
+    for b in range(NB):
+        xT[b] = stage[b].T
+    cot_in = [pltpu.make_async_copy(cot.at[b], stage.at[b], dms.at[b]) for b in range(NB)]
+    for copy in cot_in:
+        copy.start()
+    A.step(0)
+    B.step(0)
+    halo[1].start()
+    T.start(0)
+    for b in range(NB):
+        set_bias(b)
+    A.step(1)
+    B.step(1)
+    O.start(0)
+    for copy in cot_in:
+        copy.wait()
+    for b in range(NB):
+        coT[b] = stage[b].T
+    A.step(2)
+    B.step(2)
+    I.start(0)
+    U.start(0)
+    A.step(3)
+    B.step(3)
+    T.step(0)
+    O.step(0)
+
+    again = bufA[..., 768:896].reshape(D, 128)[:, 0:1].astype(f32)
+
+    def w3(p):
+        at = (p % 2) * 384
+        return (bufA if p < 2 else bufB)[..., at : at + 384].reshape(D, 384)
+
+    def own_proj(b):
+        X = xT[b].astype(f32)
+        niO[b] = (X * norm_scale(X) * again).astype(bf16)
+        for p in range(PAIRS):
+            w = w3(p)
+            kvO[b, p] = mm(niO[b], w[:, 128:384], 0, 0).astype(bf16)
+            qs[b, p] = mm(w[:, 0:128], niO[b], 0, 0).astype(bf16) * jnp.asarray(0.125, bf16)
+
+    def prev_proj(b):
+        X = tokP[b].T.astype(f32)
+        niP[b] = (X * norm_scale(X) * again).astype(bf16)
+        for p in range(PAIRS):
+            kvP[b, p] = mm(niP[b], w3(p)[:, 128:384], 0, 0).astype(bf16)
+
+    def attend(b, p):
+        kp, vp = kvP[b, p, :, 0:128], kvP[b, p, :, 128:256].T
+        ko, vo = kvO[b, p, :, 0:128], kvO[b, p, :, 128:256].T
+        q2 = qs[b, p]
+        for e in range(2):
+            qz = one_head(q2, e)
+            sp = mm(kp, qz, 1, 0)
+            so = mm(ko, qz, 1, 0) + bias[b]
+            top = jnp.maximum(
+                jnp.max(so, axis=0, keepdims=True), jnp.max(sp, axis=0, keepdims=True) - away
+            )
+            ep = jnp.exp(sp - (top + away))
+            eo = jnp.exp(so - top)
+            total = jnp.sum(ep, axis=0, keepdims=True) + jnp.sum(eo, axis=0, keepdims=True)
+            rows = slice(e * HD, (e + 1) * HD)
+            o = mm(vp[rows], ep.astype(bf16), 1, 0) + mm(vo[rows], eo.astype(bf16), 1, 0)
+            loc[b, p, rows] = o / total
+            lse[b, 2 * p + e] = top + jnp.log(total)
+
+    def attend_loop(b, lo, hi):
+        def body(p, carry):
+            attend(b, p)
+            return carry
+
+        lax.fori_loop(lo, hi, body, 0)
+
+    def remember(b):
+        table = bufT[...].reshape(-1, D)
+        q = qs[b].reshape(D, SEG).astype(f32)
+        row = lax.broadcasted_iota(jnp.int32, (table.shape[0], SEG), 0)
+        scores = []
+        for k in range(KNN):
+            hot = (row == nbr[b, k : k + 1, :]).astype(bf16)
+            rows = mm(table, hot, 0, 0)
+            near[b, k] = rows.astype(bf16)
+            scores.append(per_head(q * rows))
+        top = scores[0]
+        for k in range(1, KNN):
+            top = jnp.maximum(top, scores[k])
+        scores = [jnp.exp(v - top) for v in scores]
+        total = scores[0] + scores[1] + scores[2] + scores[3]
+        for k in range(KNN):
+            nw[b, k] = scores[k] / total
+
+    def blend(b):
+        cols = bufO[..., 512:640].reshape(D, 128).astype(f32)
+        gvec, fgain = cols[:, 1:2], cols[:, 2:3]
+        recalled = spread(nw[b, 0]) * near[b, 0].astype(f32)
+        for k in range(1, KNN):
+            recalled = recalled + spread(nw[b, k]) * near[b, k].astype(f32)
+        local = loc[b].reshape(D, SEG)
+        opened = jax.nn.sigmoid(per_head(local * gvec))
+        gate[b] = opened
+        wide = spread(opened)
+        blended = (wide * recalled + (1.0 - wide) * local).astype(bf16)
+        bld[b] = blended
+        w = bufO[..., 0:512].reshape(D, D)
+        middle = xT[b].astype(f32) + mm(w, blended, 0, 0)
+        mid[b] = middle
+        y[b] = middle
+        fi[b] = (middle * norm_scale(middle) * fgain).astype(bf16)
+
+    for b in range(NB):
+        own_proj(b)
+        if b == 0:
+            T.step(1)
+            O.step(1)
+    halo[0].wait_recv()
+    prev_proj(0)
+    T.step(2)
+    O.step(2)
+    I.step(0)
+    U.step(0)
+    attend_loop(0, 0, 2)
+    halo[1].wait_recv()
+    prev_proj(1)
+    O.step(3)
+    attend_loop(0, 2, 4)
+    remember(0)
+    blend(0)
+    I.step(1)
+    U.step(1)
+    attend_loop(1, 0, 2)
+    I.step(2)
+    U.step(2)
+    attend_loop(1, 2, 4)
+    remember(1)
+    blend(1)
+    I.step(3)
+    U.step(3)
+    for g in ag:
+        g.drain()
+    for copy in halo:
+        copy.wait_send()
+
+    root = 0.7978845608028654
+    RI = Scatter(place, bufI, (rI0, rI1, rI2, rI3), rss.at[0], rsr.at[0], ("c", "x", "y"))
+    RU = Scatter(place, bufU, (rU0, rU1, rU2, rU3), rss.at[1], rsr.at[1], ("c", "y", "x"))
+    RO = Scatter(place, bufO, (rO0, rO1, rO2, rO3), rss.at[2], rsr.at[2], ("c", "x", "y"))
+    RQ = [
+        Scatter(
+            place,
+            accQ.at[p],
+            (rQ0.at[p], rQ1.at[p], rQ2.at[p], rQ3.at[p]),
+            rss.at[3 + p],
+            rsr.at[3 + p],
+            ("c", "x", "y") if p % 2 else ("c", "y", "x"),
+        )
+        for p in range(PAIRS)
+    ]
+
+    for j in range(4):
+        lanes = slice(j * 512, (j + 1) * 512)
+        win = bufI[..., lanes].reshape(D, 512)
+        wout = bufU[j].reshape(512, D)
+        gin = None
+        for b in range(NB):
+            v = mm(win, fi[b], 0, 0)
+            gh = mm(wout, coT[b], 1, 0)
+            v2 = v * v
+            t = jnp.tanh(root * v * (1.0 + 0.044715 * v2))
+            half = 0.5 * (1.0 + t)
+            hb = (v * half).astype(bf16)
+            slope = half + 0.5 * v * (1.0 - t * t) * (root * (1.0 + 3 * 0.044715 * v2))
+            gp = (gh * slope).astype(bf16)
+            y[b] = y[b] + mm(wout, hb, 0, 0)
+            back_in = mm(win, gp, 1, 0)
+            if j == 0:
+                gm[b] = back_in
+            else:
+                gm[b] = gm[b] + back_in
+            a = mm(hb, coT[b], 1, 1)
+            c = mm(fi[b], gp, 1, 1)
+            if b == 0:
+                gout, gin = a, c
+            else:
+                gout, gin = gout + a, gin + c
+        bufU[j] = gout.astype(bf16).reshape(2, 2, 2, 64, D)
+        bufI[..., lanes] = gin.astype(bf16).reshape(dpn, 2, 2, 2, 16, 512)
+    RI.start(0)
+    RU.start(0)
+
+    out_copies = []
+    cols = bufO[..., 512:640].reshape(D, 128).astype(f32)
+    gvec, fgain = cols[:, 1:2], cols[:, 2:3]
+    wout_a = bufO[..., 0:512].reshape(D, D)
+    gwo = None
+    ggv = None
+    for b in range(NB):
+        stage[b] = y[b].astype(bf16).T
+        copy = pltpu.make_async_copy(stage.at[b], out.at[b], dms.at[b])
+        copy.start()
+        out_copies.append(copy)
+        middle = mid[b]
+        scale = norm_scale(middle)
+        grad = coT[b].astype(f32) + norm_back(gm[b] * fgain, middle * scale, scale)
+        gm[b] = grad
+        gb = grad.astype(bf16)
+        part = mm(bld[b], gb, 1, 1)
+        gwo = part if gwo is None else gwo + part
+        gbl = mm(wout_a, gb, 1, 0)
+        local = loc[b].reshape(D, SEG)
+        opened = gate[b]
+        along = per_head(gbl * local)
+        hits = [per_head(gbl * near[b, k].astype(f32)) for k in range(KNN)]
+        mixed = hits[0] * nw[b, 0]
+        for k in range(1, KNN):
+            mixed = mixed + hits[k] * nw[b, k]
+        ggate = (mixed - along) * opened * (1.0 - opened)
+        wide = spread(ggate)
+        part = jnp.sum(wide * local, axis=1, keepdims=True)
+        ggv = part if ggv is None else ggv + part
+        dlo = (spread(1.0 - opened) * gbl + wide * gvec).astype(bf16)
+        fi[b] = dlo
+        dots = per_head(dlo.astype(f32) * local)
+        for h in range(HEADS):
+            dlt[b, h] = dots[h : h + 1, :]
+        dq = None
+        for k in range(KNN):
+            weight = spread(nw[b, k] * opened * (hits[k] - mixed) * 0.125)
+            part = weight * near[b, k].astype(f32)
+            dq = part if dq is None else dq + part
+        y[b] = dq
+    bufO[..., 0:512] = gwo.astype(bf16).reshape(dpn, 2, 2, 2, 16, 512)
+    bufO[..., 512:640] = jnp.broadcast_to(ggv, (D, 128)).astype(bf16).reshape(dpn, 2, 2, 2, 16, 128)
+    RO.start(0)
+
+    def retreat(b, p, kv, own):
+        k2, v2 = kv[b, p, :, 0:128], kv[b, p, :, 128:256]
+        kt = k2.T
+        q2 = qs[b, p]
+        d2 = fi[b, pl.ds(p * 128, 128), :]
+        for e in range(2):
+            rows = slice(e * HD, (e + 1) * HD)
+            sc = mm(k2, one_head(q2, e), 1, 0)
+            if own:
+                pr = jnp.exp((sc + bias[b]) - lse[b, 2 * p + e])
+            else:
+                pr = jnp.exp(sc - (lse[b, 2 * p + e] + away))
+            dpr = mm(v2, one_head(d2, e), 1, 0)
+            ds = (pr * (dpr - dlt[b, 2 * p + e])).astype(bf16)
+            dv = mm(d2[rows], pr.astype(bf16), 1, 1).astype(bf16)
+            dk = mm(q2[rows], ds, 1, 1).astype(bf16)
+            dq = mm(kt[rows], ds, 1, 0) * 0.125
+            at = pl.ds(p * 128 + e * HD, HD)
+            if own:
+                G3[b, p, e * HD : (e + 1) * HD] = (y[b, at, :] + dq).astype(bf16)
+                G3[b, p, 128 + e * HD : 128 + (e + 1) * HD] = dk
+                G3[b, p, 256 + e * HD : 256 + (e + 1) * HD] = dv
+            else:
+                y[b, at, :] = y[b, at, :] + dq
+                Gp[b, p, e * HD : (e + 1) * HD] = dk
+                Gp[b, p, 128 + e * HD : 128 + (e + 1) * HD] = dv
+
+    for b in range(NB):
+
+        def body(p, carry):
+            retreat(b, p, kvP, False)
+            return carry
+
+        lax.fori_loop(0, PAIRS, body, 0)
+        sent = mm(w3(0)[:, 128:384], Gp[b, 0], 1, 0)
+        for p in range(1, PAIRS):
+            sent = sent + mm(w3(p)[:, 128:384], Gp[b, p], 1, 0)
+        tokP[b] = sent.astype(bf16)
+        back[b].start()
+        if b == 0:
+            RI.step(0)
+            RU.step(0)
+            RO.step(0)
+        else:
+            RI.step(1)
+            RU.step(1)
+            RO.step(1)
+
+    for p in range(PAIRS):
+
+        def body(b, carry):
+            retreat(b, p, kvO, True)
+            return carry
+
+        body(0,0);body(1,0)
+        quer = mm(niO[0], G3[0, p, 0:128], 1, 1) + mm(niO[1], G3[1, p, 0:128], 1, 1)
+        accQ[p, ..., 0:128] = quer.astype(bf16).reshape(dpn, 2, 2, 2, 16, 128)
+        rest = mm(niO[0], G3[0, p, 128:384], 1, 1)
+        rest = rest + mm(niP[0], Gp[0, p], 1, 1)
+        rest = rest + mm(niO[1], G3[1, p, 128:384], 1, 1)
+        rest = rest + mm(niP[1], Gp[1, p], 1, 1)
+        accQ[p, ..., 128:384] = rest.astype(bf16).reshape(dpn, 2, 2, 2, 16, 256)
+        RQ[p].start(0)
+        if p == 0:
+            RI.step(2)
+            RU.step(2)
+            RO.step(2)
+        if p == 1:
+            RQ[0].step(0)
+            gi[...] = RI.total()
+            gu[...] = RU.total()
+            last = RO.total()
+        if p == 2:
+            RQ[0].step(1)
+            RQ[1].step(0)
+        if p == 3:
+            RQ[0].step(2)
+            RQ[1].step(1)
+            RQ[2].step(0)
+
+    def finish(b):
+        total = mm(w3(0), G3[b, 0], 1, 0)
+        for p in range(1, PAIRS):
+            total = total + mm(w3(p), G3[b, p], 1, 0)
+        total = total + hgR[b].astype(f32)
+        X = xT[b].astype(f32)
+        scale = norm_scale(X)
+        res = gm[b] + norm_back(total * again, X * scale, scale)
+        mid[b] = res.T
+        copy = pltpu.make_async_copy(mid.at[b], ig.at[b], dms.at[2 + b])
+        copy.start()
+        return copy
+
+    RQ[3].step(0)
+    back[0].wait_recv()
+    copy0 = finish(0)
+    RQ[1].step(2)
+    RQ[2].step(1)
+    RQ[3].step(1)
+    back[1].wait_recv()
+    copy1 = finish(1)
+    RQ[2].step(2)
+    RQ[3].step(2)
+    go_[...] = last[:, 0:512]
+    own = gains[...].astype(f32)
+    fsum = jnp.sum(gi[...] * wi[...].astype(f32), axis=1, keepdims=True) / own[:, 2:3]
+    for p in range(PAIRS):
+        res = RQ[p].total()
+        gq[:, p * 128 : (p + 1) * 128] = res[:, 0:128]
+        gk[:, p * 128 : (p + 1) * 128] = res[:, 128:256]
+        gv[:, p * 128 : (p + 1) * 128] = res[:, 256:384]
+    asum = (
+        gq[...] * wq[...].astype(f32) + gk[...] * wk[...].astype(f32) + gv[...] * wv[...].astype(f32)
+    )
+    asum = jnp.sum(asum, axis=1, keepdims=True) / own[:, 0:1]
+    lane = lax.broadcasted_iota(jnp.int32, (16, 128), 1)
+    gg[...] = jnp.where(lane == 0, asum, jnp.where(lane == 1, last[:, 513:514], fsum))
+    for r in [RI, RU, RO] + RQ:
+        r.drain()
+    for copy in back:
+        copy.wait_send()
+    for copy in out_copies + [copy0, copy1]:
+        copy.wait()
+
+
+def fused(dpn, tokens, prefix, neighbours, table, attn_gain, w_query, w_key, w_value, gate_vector,
+          w_output, ffn_gain, w_inner, w_outer, cotangent):
+    gains = jnp.pad(jnp.stack([attn_gain, gate_vector, ffn_gain], axis=1), ((0, 0), (0, 125)))
+    vm = pl.BlockSpec(memory_space=pltpu.VMEM)
+    hb = pl.BlockSpec(memory_space=pl.ANY)
+    sm = pl.BlockSpec(memory_space=pltpu.SMEM)
+    V = pltpu.VMEM
+    lead = (dpn, 2, 2, 2)
+    sq = (NB, D, SEG)
+
+    def recvs(rows, cols, pre=()):
+        return [
+            V(pre + (dpn, 2, 2, rows, cols), bf16),
+            V(pre + (dpn, 2, rows, cols), bf16),
+            V(pre + (dpn, rows, cols), bf16),
+            V(pre + (dpn - 1, rows, cols), bf16),
+        ]
+
+    scratch = [
+        V(lead + (16, 896), bf16),
+        V(lead + (16, 768), bf16),
+        V(lead + (16, 640), bf16),
+        V(lead + (16, FF), bf16),
+        V(lead + (64, D), bf16),
+        V((2, 2, 2) + table.shape, bf16),
+        V(sq, bf16),
+        V(sq, bf16),
+        V(sq, bf16),
+        V(sq, bf16),
+        V(sq, bf16),
+        V(sq, bf16),
+        V((NB, PAIRS, 128, SEG), bf16),
+        V((NB, PAIRS, SEG, 256), bf16),
+        V((NB, PAIRS, SEG, 256), bf16),
+        V((NB, PAIRS, 128, SEG), f32),
+        V((NB, KNN, D, SEG), bf16),
+        V((NB, KNN, HEADS, SEG), f32),
+        V((NB, HEADS, SEG), f32),
+        V((NB, HEADS, 1, SEG), f32),
+        V((NB, HEADS, 1, SEG), f32),
+        V(sq, f32),
+        V(sq, bf16),
+        V(sq, bf16),
+        V(sq, f32),
+        V(sq, f32),
+        V((NB, SEG, SEG), f32),
+        V((NB, PAIRS, 384, SEG), bf16),
+        V((NB, PAIRS, 256, SEG), bf16),
+        V((PAIRS,) + lead + (16, 384), bf16),
+        V(sq, bf16),
+    ]
+    scratch += recvs(16, FF) + recvs(64, D) + recvs(16, 640) + recvs(16, 384, (PAIRS,))
+    dma = pltpu.SemaphoreType.DMA
+    scratch += [
+        dma((6, dpn + 2)), dma((6, dpn + 2)), dma((7, dpn + 2)), dma((7, dpn + 2)), dma((4,)), dma((4,)), dma((4,)),
+    ]
+    rows = w_query.shape[0]
+    sds = jax.ShapeDtypeStruct
+    out = pl.pallas_call(
+        lambda *refs: layer(dpn, *refs),
+        name="layer",
+        out_shape=(
+            sds(tokens.shape, bf16),
+            sds(tokens.shape, f32),
+            sds((rows, D), f32),
+            sds((rows, D), f32),
+            sds((rows, D), f32),
+            sds((rows, D), f32),
+            sds((rows, FF), f32),
+            sds(w_outer.shape, f32),
+            sds((rows, 128), f32),
+        ),
+        in_specs=[hb, sm, vm, vm, vm, vm, vm, vm, vm, vm, vm, hb],
+        out_specs=(hb, hb) + (vm,) * 7,
+        scratch_shapes=scratch,
+        compiler_params=pltpu.CompilerParams(
+            collective_id=0, has_side_effects=True, vmem_limit_bytes=63 * 2**20
+        ),
+    )(
+        tokens, prefix, neighbours.transpose(0, 2, 1), table, gains, w_query, w_key, w_value, w_output,
+        w_inner, w_outer, cotangent,
+    )
+    return (
+        out[0], out[1], out[8][:, 0], out[2], out[3], out[4], out[8][:, 1], out[5], out[8][:, 2], out[6], out[7],
+    )
+
+
 masked_floor = -1000000000.0
 
 
@@ -44,7 +730,7 @@
     return lax.rsqrt(jnp.mean(values * values, axis=-1, keepdims=True) + epsilon)
 
 
-def norm_back(grad_normed, normed, scale):
+def norm_back_rows(grad_normed, normed, scale):
     return scale * (grad_normed - normed * jnp.mean(grad_normed * normed, axis=-1, keepdims=True))
 
 
@@ -187,7 +873,7 @@
     grad_inner = times_first_t(ffn_in, grad_pre)
     grad_ffn_in = times_second_t(grad_pre, w_inner)
     grad_ffn_gain = jnp.sum(grad_ffn_in * normed_two, axis=0)
-    grad_middle = dout + norm_back(
+    grad_middle = dout + norm_back_rows(
         grad_ffn_in * ffn_gain.astype(jnp.float32), normed_two, scale_two
     )
     grad_branch_b = grad_middle.astype(jnp.bfloat16)
@@ -263,7 +949,7 @@
         + times_second_t(grad_value_b, w_value)
     )
     grad_attn_gain = jnp.sum(grad_normed_in * normed_one, axis=0)
-    input_grad = grad_middle + norm_back(
+    input_grad = grad_middle + norm_back_rows(
         grad_normed_in * attn_gain.astype(jnp.float32), normed_one, scale_one
     )
     grads = (
@@ -280,7 +966,7 @@
     return (grads, input_grad)
 
 
-def local(
+def plain(
     tokens,
     prefix,
     neighbours,
@@ -338,37 +1024,22 @@
 
 
 def solution(mesh):
+    dpn = mesh.shape["dp"]
+
+    def local(*args):
+        if mesh.shape["seq"] == 8 and args[5].shape[0] == 16:
+            return fused(dpn, *args)
+        return plain(*args)
+
+    rows = P(("dp", "seq"))
+    wide = P(("dp", "seq"), None)
+    block = P("dp", "seq", None)
     return jax.shard_map(
         local,
         mesh=mesh,
         in_specs=(
-            P("dp", "seq", None),
-            P("dp"),
-            P("dp", "seq", None),
-            P("seq", None),
-            P(("dp", "seq")),
-            P(("dp", "seq"), None),
-            P(("dp", "seq"), None),
-            P(("dp", "seq"), None),
-            P(("dp", "seq")),
-            P(("dp", "seq"), None),
-            P(("dp", "seq")),
-            P(("dp", "seq"), None),
-            P(("dp", "seq"), None),
-            P("dp", "seq", None),
+            block, P("dp"), block, P("seq", None), rows, wide, wide, wide, rows, wide, rows, wide, wide, block,
         ),
-        out_specs=(
-            P("dp", "seq", None),
-            P("dp", "seq", None),
-            P(("dp", "seq")),
-            P(("dp", "seq"), None),
-            P(("dp", "seq"), None),
-            P(("dp", "seq"), None),
-            P(("dp", "seq")),
-            P(("dp", "seq"), None),
-            P(("dp", "seq")),
-            P(("dp", "seq"), None),
-            P(("dp", "seq"), None),
-        ),
+        out_specs=(block, block, rows, wide, wide, wide, rows, wide, rows, wide, wide),
         check_vma=False,
     )

time: 1380 us -> 188 us (0.14)
  waiting for transfers between devices: 578 us -> 0 us
  matrix products: 293 us -> 0 us
  blocking collectives: 253 us -> 0 us
  Pallas kernels: 0 us -> 173 us
  local copies, waits for them, and re-layouts: 116 us -> 9.69 us
  other arithmetic: 99 us -> 0.7 us
  starting transfers between devices: 18 us -> 0 us
  between operations: 15.4 us -> 0.92 us
    reduce_scatter x6 -> x0, waiting for transfers between devices: 560 us -> none  [local(): lax.psum_scatter(running, ('dp', 'seq'), scatter_dimension=0, tiled=True)]
    dot_general x148 -> x0, matrix products: 293 us -> none  [the longest x60 110 us: times_second_t(): lax.dot_general(left, right, (((1,), (1,)), ((), ())), preferred_element_...]
    pallas_call x0 -> x1, Pallas kernels: none -> 173 us  [fused(): pl.pallas_call(lambda *refs: layer(dpn, *refs), name='layer', out_shape=(...]
    all_gather x4 -> x0, blocking collectives: 162 us -> none  [the longest x1 42.1 us: fetch_attention(): lax.all_gather(w_key, ('dp', 'seq'), axis=0, tiled=True)]
    unnamed x2 -> x0, blocking collectives: 90.8 us -> none
    unnamed x8 -> x0, other arithmetic: 50.3 us -> none
    unnamed x197 -> x22, local copies, waits for them, and re-layouts: 37.8 us -> 7.38 us
    reduce_sum x26 -> x0, other arithmetic: 26.1 us -> none  [the longest x16 17.3 us: head_forward(): row_sum = jnp.sum(exponent, axis=1, keepdims=True)]
  transfers between devices with their start and end apart: 17 -> 0, of which waited for: 8 -> 0; matrix products, arithmetic and copies ran while one was open for 35% -> 0% of each run, Pallas kernels for 0% -> 0%
where the time goes in v1:
time: 188 us; the launch traced here: 184 us
  Pallas kernels  173 us (92%)
  local copies, waits for them, and re-layouts  9.69 us (5%)
    pallas_call x1, Pallas kernels, fused(): pl.pallas_call(lambda *refs: layer(dpn, *refs), name='layer', out_shape=(...  173 us
    unnamed x22, local copies, waits for them, and re-layouts  7.38 us

profile of v1, /device:TPU:0, one launch (start us, length us, event | category | flops | bytes accessed | tf_op | source)
XLA Modules:
  0.0 184.0 jit_solution(9551259912500383791)
XLA Ops:
  0.6 0.7 pad_maximum_fusion
  1.3 0.1 copy.31
  1.4 0.6 pad.4.refs_4_
  2.0 172.6 %layer.1 = (bf16[2,512,512]{2,1,0:T(8,128)(2,1)}, f32[2,512,512]{2,1,0:T(8,128)}, f32[16,512]{1,0:T(8,128)}, f32[16,512]{1,0:T(8,128)}, f32[16,512]{1,0:T(8,128)...) custom-call(bf16[2,512,512]{2,1,0:T(8,128)(2,1)} %refs_0_.1, s32[2]{0:T(128)} %refs_1_.1, ...), custom_call_target="tpu_custom_call" | custom-call | tf_op jit(solution)/shard_map/layer/pallas_call | solution.py:671
  174.7 0.0 copy-start
  174.7 1.6 slice_reduce_fusion
  176.3 2.3 %copy.40 = bf16[2,512,512]{2,1,0:T(8,128)(2,1)} copy(bf16[2,512,512]{2,1,0:T(8,128)(2,1)} %get-tuple-element.43) | data formatting | bytes 2097152
  178.6 0.0 copy-done
  178.6 0.0 copy-start.6
  178.6 0.0 copy-start.5
  178.6 0.0 copy-start.4
  178.6 0.0 copy-start.3
  178.6 0.0 copy-start.2
  178.6 0.0 copy-start.1
  178.6 1.3 copy.41
  179.9 0.0 copy-done.6
  179.9 0.6 copy.42
  180.6 0.0 copy-done.5
  180.6 0.6 copy.43
  181.2 0.0 copy-done.4
  181.2 0.6 copy.44
  181.8 0.0 copy-done.3
  181.8 0.6 copy.45
  182.4 0.0 copy-done.2
  182.4 0.7 copy.46
  183.1 0.0 copy-done.1
  183.1 0.7 copy.47
Async XLA Ops:
  174.7 3.9 %copy-start = (f32[2,512,512]{2,1,0:T(8,128)S(1)}, f32[2,512,512]{2,1,0:T(8,128)}, u32[]{:S(2)}) copy-start(f32[2,512,512]{2,1,0:T(8,128)} %get-tuple-element.44) | copy-start | bytes 6291460
  178.6 1.4 copy-start.6
  178.6 2.0 %copy-start.5 = (f32[16,512]{1,0:T(8,128)S(1)}, f32[16,512]{1,0:T(8,128)}, u32[]{:S(2)}) copy-start(f32[16,512]{1,0:T(8,128)} %get-tuple-element.47) | copy-start | bytes 98308
  178.6 2.6 %copy-start.4 = (f32[16,512]{1,0:T(8,128)S(1)}, f32[16,512]{1,0:T(8,128)}, u32[]{:S(2)}) copy-start(f32[16,512]{1,0:T(8,128)} %get-tuple-element.48) | copy-start | bytes 98308
  178.6 3.2 %copy-start.3 = (f32[16,512]{1,0:T(8,128)S(1)}, f32[16,512]{1,0:T(8,128)}, u32[]{:S(2)}) copy-start(f32[16,512]{1,0:T(8,128)} %get-tuple-element.50) | copy-start | bytes 98308
  178.6 3.8 %copy-start.2 = (f32[16,2048]{1,0:T(8,128)S(1)}, f32[16,2048]{1,0:T(8,128)}, u32[]{:S(2)}) copy-start(f32[16,2048]{1,0:T(8,128)} %get-tuple-element.52) | copy-start | bytes 393220
  178.6 4.5 %copy-start.1 = (f32[64,512]{1,0:T(8,128)S(1)}, f32[64,512]{1,0:T(8,128)}, u32[]{:S(2)}) copy-start(f32[64,512]{1,0:T(8,128)} %get-tuple-element.53) | copy-start | bytes 393220
